TPU v7x, 256 devices: a whole 4x4x8 slice. The times are simulated.
256 devices in a mesh: leaf: 8 (over z_hi, x), row: 4 (over y), col: 8 (over z_lo, core).
Axes of the slice: x: 4, y: 4, z: 8 (z_hi: 2, z_lo: 4; z = z_hi * 4 + z_lo), core: 2. Of those that a mesh axis runs over, the one named last changes fastest.
Arguments:
- sigma_root: float32 [8192, 8192], P('leaf', ('row', 'col')), as said below
- structure: int32 [16, 1024], replicated, may hold values from 0 to 8191, as said below
- inv_diag: float32 [16, 2048, 2048], P('leaf', 'row', 'col'), as said below
- panel: float32 [16, 1024, 2048], P('leaf', None, 'row'), may hold values from -0.1875 to 0.1875
Outputs:
- sigma_panel: float32 [16, 1024, 2048], P('leaf', 'row', 'col')
- sigma_diag: float32 [16, 2048, 2048], P('leaf', 'row', 'col')
Inputs may be any that keep to these rules, and one draw needn't show every extreme that they name: structure[h] is increasing, and of the root indices in each aligned block of 32, exactly 4 appear in structure[h]. sigma_root is symmetric. inv_diag[h] is lower triangular with a positive diagonal.
All inputs are finite; a program needn't handle non-finite values.
Results may differ from a plain program's by a relative error of at most 0.0003.
Values sent between devices are 32-bit elements; how exact they have to be, the bound alone decides.
A program may use at most 128 MiB of HBM per device.

v0:
```python
from functools import partial

import jax
import jax.numpy as jnp
from jax import lax
from jax.sharding import PartitionSpec as P


def pick_block(source, row_index, col_index):
    return jnp.take(jnp.take(source, row_index, axis=0), col_index, axis=1)


def body(sigma_root, structure, inv_diag, panel):
    leaf_pos = lax.axis_index("leaf")
    row_pos = lax.axis_index("row")
    col_pos = lax.axis_index("col")
    row_count = lax.axis_size("row")
    col_count = lax.axis_size("col")
    block_rows, block_cols = sigma_root.shape
    per_group = inv_diag.shape[0]
    struct_len = structure.shape[1]
    col_share = struct_len // (row_count * col_count)
    grid_pos = row_pos * col_count + col_pos
    col_index = (
        lax.dynamic_slice_in_dim(structure, grid_pos * col_share, col_share, 1)
        - grid_pos * block_cols
    )
    stripe = lax.all_gather(sigma_root, "leaf", axis=0, tiled=True)
    own_rows = lax.dynamic_slice_in_dim(structure, leaf_pos * per_group, per_group, 0)
    own_cols = lax.dynamic_slice_in_dim(col_index, leaf_pos * per_group, per_group, 0)
    pieces = jax.vmap(partial(pick_block, stripe))(own_rows, own_cols)
    ancestor = lax.all_gather(pieces, "col", axis=2, tiled=True)
    partial_product = jnp.einsum(
        "msk,mkj->msj",
        panel,
        inv_diag,
        precision=lax.Precision.HIGHEST,
        preferred_element_type=jnp.float32,
    )
    product = lax.psum(partial_product, "row")
    sigma_panel = -jnp.einsum(
        "mts,mtj->msj",
        ancestor,
        product,
        precision=lax.Precision.HIGHEST,
        preferred_element_type=jnp.float32,
    )
    share_rows = struct_len // row_count
    product_rows = lax.dynamic_slice_in_dim(product, row_pos * share_rows, share_rows, 1)
    left_terms = jnp.concatenate([inv_diag, product_rows], axis=1)
    right_terms = jnp.concatenate([inv_diag, -sigma_panel], axis=1)
    partials = jnp.einsum(
        "mkn,mkj->mnj",
        lax.all_gather(left_terms, "col", axis=2, tiled=True),
        right_terms,
        precision=lax.Precision.HIGHEST,
        preferred_element_type=jnp.float32,
    )
    sigma_diag = lax.psum_scatter(partials, "row", scatter_dimension=1, tiled=True)
    return (sigma_panel, sigma_diag)


def solution(mesh):
    placed = (P("leaf", ("row", "col")), P(), P("leaf", "row", "col"), P("leaf", None, "row"))
    return jax.shard_map(
        body,
        mesh=mesh,
        in_specs=placed,
        out_specs=(P("leaf", "row", "col"), P("leaf", "row", "col")),
        check_vma=False,
    )
```

profile of v0, /device:TPU:231, one launch (start us, length us, event | category | flops | bytes accessed | tf_op | source)
XLA Modules:
  0.0 439.1 jit_solution(18236090330356949555)
XLA Ops:
  8.0 0.7 all-gather.4.cloned.1.call-update
  8.7 0.0 all-reduce.2.cloned.1.call-start
  8.8 7.5 %fusion.7 = f32[2,1024,256]{2,1,0:T(8,128)} fusion(f32[2,1024,512]{2,1,0:T(8,128)} %param.7, f32[2,512,256]{2,1,0:T(8,128)} %param.6), kind=kOutput, calls=%fused_computation.20 | convolution fusion | flops 3221225472 | bytes 7340032 | tf_op jit(solution)/shard_map/msk,mkj->msj/dot_general | solution.py:33
  16.3 0.0 all-gather.6.cloned.1.call-start
  16.4 0.8 compare_and_fusion.1
  17.2 0.1 reshape.22
  17.2 0.8 compare_and_fusion
  18.0 0.8 fusion.4
  18.8 151.3 %all-gather.4.cloned.1.call-done = f32[8192,256]{1,0:T(8,128)} async-done(((f32[1024,256]{1,0:T(8,128)}), f32[8192,256]{1,0:T(8,128)}) %all-gather.4.cloned.1.call-update) | async-done | bytes 8388624 | tf_op jit(solution)/shard_map/all_gather | solution.py:28
  170.1 10.0 %gather_fusion = f32[2048,256]{1,0:T(8,128)S(1)} fusion(f32[8192,256]{1,0:T(8,128)} %all-gather.4.cloned.1.call-done, s32[2048]{0:T(1024)S(1)} %bitcast_clamp_fusion), kind=kCustom, calls=%fused_computation | custom fusion | bytes 4202496 | tf_op jit(solution)/shard_map/vmap(jit(_take))/gather | solution.py:10
  180.2 1.8 copy.6
  182.0 1.8 broadcast_select_fusion
  183.8 1.0 gather_fusion.1
  184.9 0.8 select_bitcast_fusion
  185.7 0.3 copy.7
  186.1 1.1 constant_dynamic-slice_fusion
  187.2 0.2 copy.8
  187.4 1.3 pad_maximum_fusion
  188.7 0.2 reduce-scatter.2.cloned.1.call-start
  188.9 45.7 %all-gather.6.cloned.1.call-done = f32[2,1024,256]{1,2,0:T(8,128)} async-done(((f32[2,1024,32]{1,2,0:T(8,128)}), f32[2,1024,256]{1,2,0:T(8,128)}) %all-gather.6.cloned.1.call-update) | async-done | bytes 2097168 | tf_op jit(solution)/shard_map/all_gather | solution.py:32
  234.7 5.1 %fusion.6 = (f32[2,256,256]{2,1,0:T(8,128)}, f32[2,256,256]{2,1,0:T(8,128)S(1)}) fusion(f32[2,1024,256]{1,2,0:T(8,128)} %all-gather.6.cloned.1.call-done, f32[2,1024,256]{2,1,0:T(8,128)} %all-reduce.2.cloned.1.call-done), kind=kOutput, calls=%fused_computation.19 | convolution fusion | flops 1610743808 | bytes 5242880 | tf_op jit(solution)/shard_map/mts,mtj->msj/dot_general | solution.py:41
  239.8 129.4 %all-gather.8.cloned.1.call-done = f32[2,768,2048]{1,2,0:T(8,128)} async-done(((f32[2,768,256]{1,2,0:T(8,128)}), f32[2,768,2048]{1,2,0:T(8,128)}) %all-gather.8.cloned.1.call-update) | async-done | bytes 12582928 | tf_op jit(solution)/shard_map/all_gather | solution.py:54
  369.2 14.5 %fusion = f32[2,2048,256]{2,1,0:T(8,128)} fusion(f32[2,768,2048]{1,2,0:T(8,128)} %all-gather.8.cloned.1.call-done, f32[2,256,256]{2,1,0:T(8,128)S(1)} %get-tuple-element.5, f32[2,512,256]{2,1,0:T(8,128)S(1)} %copy-done), kind=kOutput, calls=%fused_computation.3 | convolution fusion | flops 9664069632 | bytes 18350080 | tf_op jit(solution)/shard_map/mkn,mkj->mnj/dot_general | solution.py:52
  383.7 48.3 %reduce-scatter.2.cloned.1.call-done = f32[2,512,256]{2,1,0:T(8,128)} async-done(((f32[2,2048,256]{2,1,0:T(8,128)}), f32[2,512,256]{2,1,0:T(8,128)}) %reduce-scatter.2.cloned.1.call-update) | async-done | bytes 1048592 | tf_op jit(solution)/shard_map/reduce_scatter | solution.py:59
  (11 shorter events, 0.2 us)
Async XLA Ops:
  8.0 162.1 %all-gather.4.cloned.1.call-start = ((), (), s32[]{:S(2)}) async-start(), calls=%async_computation.1 | async-start | bytes 9437184 | tf_op jit(solution)/shard_map/all_gather | solution.py:28
  8.7 177.4 %all-reduce.2.cloned.1.call-start = ((), (), s32[]{:S(2)}) async-start(), calls=%async_computation.3 | async-start | bytes 4194304 | tf_op jit(solution)/shard_map/psum | solution.py:40
  16.3 218.4 %all-gather.6.cloned.1.call-start = ((), (), s32[]{:S(2)}) async-start(), calls=%async_computation.2 | async-start | bytes 2359296 | tf_op jit(solution)/shard_map/all_gather | solution.py:32
  183.8 1.9 copy-start
  185.7 183.5 %all-gather.8.cloned.1.call-start = ((), (), s32[]{:S(2)}) async-start(), calls=%async_computation.4 | async-start | bytes 14155776 | tf_op jit(solution)/shard_map/all_gather | solution.py:54
  188.7 243.2 %reduce-scatter.2.cloned.1.call-start = ((), (), s32[]{:S(2)}) async-start(), calls=%async_computation.5 | async-start | bytes 5242880 | tf_op jit(solution)/shard_map/reduce_scatter | solution.py:59
Sparse Core Ops, SparseCore 0:
  11.5 158.6 all-gather.3
  185.8 48.8 all-gather.5
  236.6 132.5 all-gather.7
Sparse Core Ops, SparseCore 1:
  16.4 63.9 all-reduce.1
  383.8 48.1 reduce-scatter.1
where the time goes:
time: 443 us; the launch traced here: 439 us
  waiting for transfers between devices  376 us (85%)
  matrix products  27.1 us (6%)
  between operations  15.3 us (3%)
  local copies, waits for them, and re-layouts  14.6 us (3%)
  other arithmetic  6.21 us (1%)
    all_gather x1, waiting for transfers between devices, body(): stripe = lax.all_gather(sigma_root, 'leaf', axis=0, tiled=True)  151 us
    all_gather x1, waiting for transfers between devices, body(): lax.all_gather(left_terms, 'col', axis=2, tiled=True)  129 us
    reduce_scatter x1, waiting for transfers between devices, body(): lax.psum_scatter(partials, 'row', scatter_dimension=1, tiled=True)  48.3 us
    all_gather x1, waiting for transfers between devices, body(): ancestor = lax.all_gather(pieces, 'col', axis=2, tiled=True)  45.7 us
    dot_general x1, matrix products, body(): jnp.einsum('mkn,mkj->mnj', lax.all_gather(left_terms, 'col', axis=2, tile...  14.5 us
    gather x4, local copies, waits for them, and re-layouts, pick_block(): return jnp.take(jnp.take(source, row_index, axis=0), col_index, axis=1)  13 us
  transfers between devices with their start and end apart: 5, of which 4 were waited for; matrix products, arithmetic and copies ran while one was open for 8% of the time, Pallas kernels for 0%

commit v1 on v0

v1 whole, which is shorter than its diff:
```python
import jax
import jax.numpy as jnp
from jax import lax
from jax.sharding import PartitionSpec as P

HIGHEST = lax.Precision.HIGHEST


def mm(spec, a, b):
    return jnp.einsum(spec, a, b, precision=HIGHEST, preferred_element_type=jnp.float32)


def body(sigma_root, structure, inv_diag, panel):
    leaf_pos = lax.axis_index("leaf")
    row_pos = lax.axis_index("row")
    col_pos = lax.axis_index("col")
    leaf_count = lax.axis_size("leaf")
    row_count = lax.axis_size("row")
    col_count = lax.axis_size("col")
    block_rows, block_cols = sigma_root.shape
    per_group = inv_diag.shape[0]
    children, struct_len = structure.shape
    row_share = struct_len // leaf_count
    col_share = struct_len // (row_count * col_count)
    grid_pos = row_pos * col_count + col_pos

    rows = lax.dynamic_slice_in_dim(structure, leaf_pos * row_share, row_share, 1) - leaf_pos * block_rows
    cols = lax.dynamic_slice_in_dim(structure, grid_pos * col_share, col_share, 1) - grid_pos * block_cols
    pick_col = (cols[:, :, None] == jnp.arange(block_cols)[None, None, :]).astype(jnp.float32)
    pick_row = (rows[:, None, :] == jnp.arange(block_rows)[None, :, None]).astype(jnp.float32)
    by_col = mm("htc,rc->htr", pick_col, sigma_root)
    picked = mm("htr,hrs->hts", by_col, pick_row)
    picked = picked.reshape(leaf_count, per_group, col_share, row_share)
    got = lax.all_to_all(picked, "leaf", 0, 0)
    own_anc = got.transpose(1, 2, 0, 3).reshape(per_group, col_share, struct_len)
    gathered = lax.all_gather(inv_diag, "col", axis=2, tiled=True)
    ancestor = lax.all_gather(own_anc, "col", axis=1, tiled=True)

    product = lax.psum(mm("msk,mkj->msj", panel, inv_diag), "row")
    sigma_panel = -mm("mts,msj->mtj", ancestor, product)
    panel_full = lax.all_gather(sigma_panel, "row", axis=1, tiled=True)
    right = inv_diag - mm("msk,msj->mkj", panel, panel_full)
    partials = mm("mkn,mkj->mnj", gathered, right)
    sigma_diag = lax.psum_scatter(partials, "row", scatter_dimension=1, tiled=True)
    return (sigma_panel, sigma_diag)


def solution(mesh):
    placed = (P("leaf", ("row", "col")), P(), P("leaf", "row", "col"), P("leaf", None, "row"))
    return jax.shard_map(
        body,
        mesh=mesh,
        in_specs=placed,
        out_specs=(P("leaf", "row", "col"), P("leaf", "row", "col")),
        check_vma=False,
    )
```

time: 443 us -> 287 us (0.65)
  waiting for transfers between devices: 376 us -> 213 us
  blocking collectives: 0 us -> 12.8 us
  local copies, waits for them, and re-layouts: 14.6 us -> 3.27 us
  matrix products: 27.1 us -> 36.9 us
  other arithmetic: 6.21 us -> 1.48 us
    all_gather x3, waiting for transfers between devices: 326 us -> 119 us  [the longest x1 86.5 us: body(): gathered = lax.all_gather(inv_diag, 'col', axis=2, tiled=True)]
    psum x1, waiting for transfers between devices: 0.03 us -> 45 us  [body(): product = lax.psum(mm('msk,mkj->msj', panel, inv_diag), 'row')]
    gather x4 -> x0, local copies, waits for them, and re-layouts: 13 us -> none  [pick_block(): return jnp.take(jnp.take(source, row_index, axis=0), col_index, axis=1)]
    all_to_all x0 -> x1, blocking collectives: none -> 12.8 us  [body(): got = lax.all_to_all(picked, 'leaf', 0, 0)]
    dot_general x3 -> x6, matrix products: 27.1 us -> 36.9 us  [mm(): jnp.einsum(spec, a, b, precision=HIGHEST, preferred_element_type=jnp.floa...]
  transfers between devices with their start and end apart: 5 -> 5, of which waited for: 4 -> 4; matrix products, arithmetic and copies ran while one was open for 8% -> 6% of each run, Pallas kernels for 0% -> 0%
where the time goes in v1:
time: 287 us; the launch traced here: 283 us
  waiting for transfers between devices  213 us (74%)
  matrix products  36.9 us (13%)
  between operations  15.3 us (5%)
  blocking collectives  12.8 us (4%)
  local copies, waits for them, and re-layouts  3.27 us (1%)
    all_gather x1, waiting for transfers between devices, body(): gathered = lax.all_gather(inv_diag, 'col', axis=2, tiled=True)  86.5 us
    reduce_scatter x1, waiting for transfers between devices, body(): lax.psum_scatter(partials, 'row', scatter_dimension=1, tiled=True)  48.5 us
    psum x1, waiting for transfers between devices, body(): product = lax.psum(mm('msk,mkj->msj', panel, inv_diag), 'row')  45 us
    dot_general x6, matrix products, mm(): jnp.einsum(spec, a, b, precision=HIGHEST, preferred_element_type=jnp.floa...  36.9 us
    all_gather x1, waiting for transfers between devices, body(): panel_full = lax.all_gather(sigma_panel, 'row', axis=1, tiled=True)  32.4 us
    all_to_all x1, blocking collectives, body(): got = lax.all_to_all(picked, 'leaf', 0, 0)  12.8 us
  transfers between devices with their start and end apart: 5, of which 4 were waited for; matrix products, arithmetic and copies ran while one was open for 6% of the time, Pallas kernels for 0%

profile of v1, /device:TPU:231, one launch (start us, length us, event | category | flops | bytes accessed | tf_op | source)
XLA Modules:
  0.0 283.2 jit_solution(8383288765136442141)
XLA Ops:
  8.0 0.0 all-reduce.2.cloned.1.call-start
  8.1 7.6 %fusion.6 = f32[2,1024,256]{2,1,0:T(8,128)} fusion(f32[2,1024,512]{2,1,0:T(8,128)} %param.7, f32[2,512,256]{2,1,0:T(8,128)} %param.6), kind=kOutput, calls=%fused_computation.14 | convolution fusion | flops 3221225472 | bytes 7340032 | tf_op jit(solution)/shard_map/msk,mkj->msj/dot_general | solution.py:10
  15.6 0.0 all-reduce.2.cloned.1.call-update
  15.6 0.0 all-gather.4.cloned.1.call-start
  15.7 0.8 dynamic-slice_subtract_fusion.1
  16.5 0.7 dynamic-slice_subtract_fusion
  17.2 1.1 fusion.3
  18.3 3.1 %fusion = f32[16,32,128]{2,1,0:T(8,128)S(1)} fusion(f32[16,32,1024]{2,1,0:T(8,128)S(1)} %fusion.3, s32[16,128]{1,0:T(8,128)S(1)} %dynamic-slice_subtract_fusion), kind=kOutput, calls=%fused_computation.1 | convolution fusion | flops 807403520 | bytes 2367488 | tf_op jit(solution)/shard_map/htr,hrs->hts/dot_general | solution.py:10
  21.4 12.8 %all_to_all.5 = f32[8,2,32,128]{3,2,1,0:T(8,128)S(1)} all-to-all(f32[8,2,32,128]{3,2,1,0:T(8,128)S(1)} %bitcast.25), channel_id=1, replica_groups=mesh['leaf'=8,'row'=4,'col'=8] {'leaf'}, dimensions={0} | all-to-all | bytes 524288 | tf_op jit(solution)/shard_map/all_to_all | solution.py:34
  34.2 0.7 copy_bitcast_fusion
  34.9 0.0 all-gather.4.cloned.1.call-update
  35.0 0.0 all-gather.6.cloned.1.call-start
  35.0 45.0 %all-reduce.2.cloned.1.call-done = f32[2,1024,256]{2,1,0:T(8,128)} async-done(((f32[2,1024,256]{2,1,0:T(8,128)}), f32[2,1024,256]{2,1,0:T(8,128)}) %all-reduce.2.cloned.1.call-update) | async-done | bytes 2097168 | tf_op jit(solution)/shard_map/psum | solution.py:39
  80.0 5.1 %convolution_negate_fusion = f32[2,256,256]{2,1,0:T(8,128)} fusion(f32[2,256,1024]{2,1,0:T(8,128)} %all-gather.4.cloned.1.call-done, f32[2,1024,256]{2,1,0:T(8,128)} %all-reduce.2.cloned.1.call-done), kind=kOutput, calls=%fused_computation.6 | convolution fusion | flops 1610743808 | bytes 4718592 | tf_op jit(solution)/shard_map/mts,msj->mtj/dot_general | solution.py:10
  85.1 0.0 all-gather.6.cloned.1.call-update
  85.1 0.0 all-gather.8.cloned.1.call-start
  85.2 0.7 all-gather.8.cloned.1.call-update
  85.9 0.2 reduce-scatter.2.cloned.1.call-start
  86.1 32.4 %all-gather.6.cloned.1.call-done = f32[2,1024,256]{2,1,0:T(8,128)} async-done(((f32[2,256,256]{2,1,0:T(8,128)}), f32[2,1024,256]{2,1,0:T(8,128)}) %all-gather.6.cloned.1.call-update) | async-done | bytes 2097168 | tf_op jit(solution)/shard_map/all_gather | solution.py:41
  118.5 9.3 %fusion.2 = f32[2,512,256]{2,1,0:T(8,128)S(1)} fusion(f32[2,512,256]{2,1,0:T(8,128)S(1)} %copy-done.1, f32[2,1024,256]{2,1,0:T(8,128)} %all-gather.6.cloned.1.call-done, f32[2,1024,512]{2,1,0:T(8,128)} %param.7), kind=kOutput, calls=%fused_computation.5 | convolution fusion | flops 3221487616 | bytes 8388608 | tf_op jit(solution)/shard_map/msk,msj->mkj/dot_general | solution.py:10
  127.8 86.5 %all-gather.8.cloned.1.call-done = f32[2,512,2048]{2,1,0:T(8,128)} async-done(((f32[2,512,256]{2,1,0:T(8,128)}), f32[2,512,2048]{2,1,0:T(8,128)}) %all-gather.8.cloned.1.call-update) | async-done | bytes 8388624 | tf_op jit(solution)/shard_map/all_gather | solution.py:36
  214.2 10.8 %convolution_bitcast_fusion = f32[2,2048,256]{1,2,0:T(8,128)} fusion(f32[2,512,256]{2,1,0:T(8,128)S(1)} %fusion.2, f32[2,512,2048]{2,1,0:T(8,128)} %all-gather.8.cloned.1.call-done), kind=kOutput, calls=%fused_computation.3 | convolution fusion | flops 6442450944 | bytes 13631488 | tf_op jit(solution)/shard_map/mkn,mkj->mnj/dot_general | solution.py:10
  225.1 48.5 %reduce-scatter.2.cloned.1.call-done = f32[2,512,256]{1,2,0:T(8,128)} async-done(((f32[2,2048,256]{1,2,0:T(8,128)}), f32[2,512,256]{1,2,0:T(8,128)}) %reduce-scatter.2.cloned.1.call-update) | async-done | bytes 1048592 | tf_op jit(solution)/shard_map/reduce_scatter | solution.py:44
  273.6 2.5 copy.8
  (6 shorter events, 0.0 us)
Async XLA Ops:
  8.0 9.2 %copy-start = (f32[1024,256]{1,0:T(8,128)S(1)}, f32[1024,256]{1,0:T(8,128)}, u32[]{:S(2)}) copy-start(f32[1024,256]{1,0:T(8,128)} %param.4) | copy-start | bytes 3145732
  8.0 72.0 %all-reduce.2.cloned.1.call-start = ((), (), s32[]{:S(2)}) async-start(), calls=%async_computation.3 | async-start | bytes 4194304 | tf_op jit(solution)/shard_map/psum | solution.py:39
  15.6 64.4 %all-gather.4.cloned.1.call-start = ((), (), s32[]{:S(2)}) async-start(), calls=%async_computation.2 | async-start | bytes 2359296 | tf_op jit(solution)/shard_map/all_gather | solution.py:37
  35.0 83.5 %copy-start.1 = (f32[2,512,256]{2,1,0:T(8,128)S(1)}, f32[2,512,256]{2,1,0:T(8,128)}, u32[]{:S(2)}) copy-start(f32[2,512,256]{2,1,0:T(8,128)} %param.6) | copy-start | bytes 3145732
  35.0 83.5 %all-gather.6.cloned.1.call-start = ((), (), s32[]{:S(2)}) async-start(), calls=%async_computation.4 | async-start | bytes 2621440 | tf_op jit(solution)/shard_map/all_gather | solution.py:41
  85.1 129.1 %all-gather.8.cloned.1.call-start = ((), (), s32[]{:S(2)}) async-start(), calls=%async_computation.5 | async-start | bytes 9437184 | tf_op jit(solution)/shard_map/all_gather | solution.py:36
  85.9 187.7 %reduce-scatter.2.cloned.1.call-start = ((), (), s32[]{:S(2)}) async-start(), calls=%async_computation.6 | async-start | bytes 5242880 | tf_op jit(solution)/shard_map/reduce_scatter | solution.py:44
Sparse Core Ops, SparseCore 0:
  15.8 64.1 all-reduce.1
  85.2 33.2 all-gather.5
  120.4 93.7 all-gather.7
  225.2 48.3 reduce-scatter.1
Sparse Core Ops, SparseCore 1:
  35.0 43.6 all-gather.3

commit v2 on v1

v2 whole, which is shorter than its diff:
```python
from functools import partial

import jax
import jax.numpy as jnp
from jax import lax
from jax.experimental import pallas as pl
from jax.experimental.pallas import tpu as pltpu
from jax.sharding import PartitionSpec as P

MESH = pl.DeviceIdType.MESH
F32 = jnp.float32
BF16 = jnp.bfloat16


def split(x):
    high = x.astype(BF16)
    return high, (x - high.astype(F32)).astype(BF16)


def split3(x):
    high = x.astype(BF16)
    rest = x - high.astype(F32)
    mid = rest.astype(BF16)
    return high, mid, (rest - mid.astype(F32)).astype(BF16)


def dot(a, b):
    return lax.dot_general(a, b, (((1,), (0,)), ((), ())), preferred_element_type=F32)


def dot_t(a, b):
    return lax.dot_general(a, b, (((1,), (1,)), ((), ())), preferred_element_type=F32)


def dot3(a, b):
    ah, al = split(a)
    bh, bl = split(b)
    return dot(ah, bh) + (dot(ah, bl) + dot(al, bh))


def kernel(
    sizes,
    w_ref, i_ref, sig_ref, st_ref, pick_ref,
    sp_ref, sd_ref,
    ig, aa, asend, yt, pp, ph, pr, pf, qt, it, nt, dp, dh, dr,
    z_ss, z_rs, b_ss, b_rs, l_ss, l_rs, p_ss, p_rs, a_ss, a_rs, s_ss, s_rs, d_ss, d_rs,
):
    leaves, rows, cols, group, ns, kb, cb, root_rows = sizes
    depth = cols // 2
    tb = ns // rows
    ra = ns // (rows * cols)
    sa = ns // leaves
    leaf = lax.axis_index("leaf")
    y = lax.axis_index("row")
    c = lax.axis_index("col")
    z = c // 2
    core = c % 2
    y_next, y_prev, y_far = (y + 1) % rows, (y + rows - 1) % rows, (y + 2) % rows
    sibling = c + 1 - 2 * core

    def copy(src, dst, ss, rs, target):
        return pltpu.make_async_remote_copy(
            src_ref=src, dst_ref=dst, send_sem=ss, recv_sem=rs, device_id=target, device_id_type=MESH
        )

    barrier = pltpu.get_barrier_semaphore()
    for target in ({"row": y_next}, {"row": y_prev}, {"col": sibling}):
        pl.semaphore_signal(barrier, inc=1, device_id=target, device_id_type=MESH)
    for d in range(1, leaves):
        pl.semaphore_signal(barrier, inc=1, device_id={"leaf": (leaf + d) % leaves}, device_id_type=MESH)

    @pl.when(z > 0)
    def _():
        pl.semaphore_signal(barrier, inc=1, device_id={"col": c - 2}, device_id_type=MESH)

    @pl.when(z < depth - 1)
    def _():
        pl.semaphore_signal(barrier, inc=1, device_id={"col": c + 2}, device_id_type=MESH)

    def view(item, slot):
        if item < group:
            return ig.at[slot, item]
        return aa.at[:, pl.ds(pl.multiple_of(slot * ra, ra), ra), :]

    def z_copy(item, way, step):
        slot = c - 2 * (step - 1) if way == 0 else c + 2 * (step - 1)
        target = c + 2 if way == 0 else c - 2
        return copy(
            view(item, slot), view(item, slot),
            z_ss.at[item, way, step - 1], z_rs.at[item, way, step - 1], {"col": target},
        )

    def z_sends(way, step):
        if way == 0:
            return jnp.logical_and(z < depth - 1, z >= step - 1)
        return jnp.logical_and(z > 0, z + step - 1 <= depth - 1)

    def z_gets(way, step):
        return z >= step if way == 0 else z + step <= depth - 1

    def b_copy(item, origin):
        slot = 2 * origin + core
        return copy(view(item, slot), view(item, slot), b_ss.at[item, origin], b_rs.at[item, origin], {"col": sibling})

    def z_start(item, way, step):
        @pl.when(z_sends(way, step))
        def _():
            z_copy(item, way, step).start()

    def z_own(item):
        z_start(item, 0, 1)
        z_start(item, 1, 1)
        b_copy(item, z).start()

    def z_relay(item, step):
        for way in range(2):
            @pl.when(z_gets(way, step))
            def _():
                origin = z - step if way == 0 else z + step
                slot = 2 * origin + core
                copy(
                    view(item, slot), view(item, slot),
                    z_ss.at[item, way, step - 1], z_rs.at[item, way, step - 1], {"col": sibling},
                ).wait_recv()
                if step < depth - 1:
                    z_start(item, way, step + 1)
                b_copy(item, origin).start()

    def z_last(item):
        for origin in range(depth):
            slot = 2 * origin + 1 - core
            copy(
                view(item, slot), view(item, slot), b_ss.at[item, origin], b_rs.at[item, origin], {"col": sibling}
            ).wait_recv()

    def z_sent(item):
        for way in range(2):
            for step in range(1, depth):
                @pl.when(z_sends(way, step))
                def _():
                    z_copy(item, way, step).wait_send()
        for origin in range(depth):
            b_copy(item, origin).wait_send()

    def rs_copies(part, half, whole, ss, rs):
        right, left = {"row": y_next}, {"row": y_prev}
        plan = (
            (part(y_far, 0), half(0), right),
            (part(y_far, 1), half(1), left),
            (part(y_next, 1), whole(0, 1), right),
            (part(y_prev, 0), whole(1, 0), left),
            (part(y_next, 0), whole(0, 0), right),
            (part(y_prev, 1), whole(1, 1), left),
        )
        return [copy(src, dst, ss.at[k], rs.at[k], target) for k, (src, dst, target) in enumerate(plan)]

    def p_part(h):
        return lambda s, k: pp.at[h, pl.ds(pl.multiple_of(s * tb + k * (tb // 2), tb // 2), tb // 2), :]

    def p_rs_copies(h):
        return rs_copies(
            p_part(h), lambda k: ph.at[h, k],
            lambda w, k: pr.at[h, w, k], p_ss.at[h], p_rs.at[h],
        )

    def d_part(h):
        return lambda s, k: dp.at[h, 2 * s + k]

    def d_rs_copies(h):
        return rs_copies(
            d_part(h), lambda k: dh.at[h, k],
            lambda w, k: dr.at[h, w, k], d_ss.at[h], d_rs.at[h],
        )

    def rs_round1(copies):
        for k in range(4):
            copies[k].start()

    def rs_round2(copies, part, half):
        copies[0].wait_recv()
        mine = part(y_next, 0)
        mine[...] = mine[...] + half(0)[...]
        copies[4].start()
        copies[1].wait_recv()
        mine = part(y_prev, 1)
        mine[...] = mine[...] + half(1)[...]
        copies[5].start()

    def rs_arrived(copies):
        for k in range(2, 6):
            copies[k].wait_recv()

    def sent(copies):
        for one in copies:
            one.wait_send()

    def ag_copies(slot, ss, rs):
        right, left = {"row": y_next}, {"row": y_prev}
        plan = (
            (slot(y, 0), right), (slot(y, 1), left), (slot(y, 1), right), (slot(y, 0), left),
            (slot(y_prev, 0), right), (slot(y_next, 1), left),
        )
        return [copy(src, src, ss.at[k], rs.at[k], target) for k, (src, target) in enumerate(plan)]

    def pf_copies(h):
        slot = lambda s, k: pf.at[h, pl.ds(pl.multiple_of(s * tb + k * (tb // 2), tb // 2), tb // 2), :]
        return ag_copies(slot, a_ss.at[h], a_rs.at[h])

    def qt_copies(h):
        slot = lambda s, k: qt.at[h, s, pl.ds(k * (cb // 2), cb // 2), :]
        return ag_copies(slot, s_ss.at[h], s_rs.at[h])

    def ag_round1(copies):
        for k in range(4):
            copies[k].start()

    def ag_round2(copies):
        copies[0].wait_recv()
        copies[4].start()
        copies[1].wait_recv()
        copies[5].start()

    def ag_arrived(copies):
        for k in range(2, 6):
            copies[k].wait_recv()

    def product_partial(h):
        @pl.loop(0, rows)
        def _(s):
            at = pl.ds(pl.multiple_of(s * tb, tb), tb)
            pp[h, at, :] = dot3(w_ref[h, at, :], i_ref[h])

    def pick():
        sig_parts = split3(sig_ref[...])
        chosen = pick_ref[...]
        yt[...] = dot_t(chosen, sig_parts[0]) + (dot_t(chosen, sig_parts[1]) + dot_t(chosen, sig_parts[2]))
        at = pl.ds(pl.multiple_of(leaf * sa, sa), sa)

        @pl.loop(0, leaves * group)
        def _(h):
            local = st_ref[h, :, at] - leaf * root_rows
            hot = jnp.where(lax.broadcasted_iota(jnp.int32, (root_rows, sa), 0) == local, 1.0, 0.0).astype(BF16)
            parts = split3(yt[pl.ds(pl.multiple_of(h * ra, ra), ra), :])
            asend[h] = dot(parts[0], hot) + (dot(parts[1], hot) + dot(parts[2], hot))

    def l_copies():
        out = []
        for d in range(1, leaves):
            target = (leaf + d) % leaves
            out.append(copy(
                asend.at[pl.ds(target * group, group)],
                aa.at[:, pl.ds(pl.multiple_of(c * ra, ra), ra), pl.ds(pl.multiple_of(leaf * sa, sa), sa)],
                l_ss.at[d - 1], l_rs.at[d - 1], {"leaf": target},
            ))
        return out

    def product_done(h):
        for k in range(2):
            at = pl.ds(pl.multiple_of(y * tb + k * (tb // 2), tb // 2), tb // 2)
            pf[h, at, :] = pp[h, at, :] + (pr[h, 0, k] + pr[h, 1, k])

    def ancestor_times(h):
        total = dot3(aa[h, :, pl.ds(0, tb)], pf[h, pl.ds(0, tb), :])
        for s in range(1, rows):
            total = total + dot3(aa[h, :, pl.ds(s * tb, tb)], pf[h, pl.ds(s * tb, tb), :])
        sp_ref[h] = -total
        qt[h, y] = total.T

    def right_terms(h):
        nt[h] = it[h] + dot3(qt[h, 0], w_ref[h, pl.ds(0, tb), :])

        @pl.loop(1, rows)
        def _(s):
            nt[h] = nt[h] + dot3(qt[h, s], w_ref[h, pl.ds(pl.multiple_of(s * tb, tb), tb), :])

    def diagonal_partial(h):
        @pl.loop(0, cols)
        def _(slot):
            dp[h, slot] = dot3(nt[h], ig[slot, h])

    def diagonal_done(h):
        for k in range(2):
            total = dp[h, 2 * y + k] + (dr[h, 0, k] + dr[h, 1, k])
            sd_ref[h, pl.ds(k * cb, cb), :] = total.T

    ig[c] = i_ref[...]
    product_partial(0)
    pl.semaphore_wait(barrier, 2 + leaves + (z > 0).astype(jnp.int32) + (z < depth - 1).astype(jnp.int32))

    anc = group
    p0, p1 = p_rs_copies(0), p_rs_copies(1)
    f0, f1 = pf_copies(0), pf_copies(1)
    q0, q1 = qt_copies(0), qt_copies(1)
    d0, d1 = d_rs_copies(0), d_rs_copies(1)
    exchange = l_copies()

    rs_round1(p0)
    z_own(0)
    pick()
    for one in exchange:
        one.start()
    aa[:, pl.ds(pl.multiple_of(c * ra, ra), ra), pl.ds(pl.multiple_of(leaf * sa, sa), sa)] = asend[
        pl.ds(leaf * group, group)
    ]
    product_partial(1)
    rs_round1(p1)
    rs_round2(p0, p_part(0), lambda k: ph.at[0, k])
    for h in range(group):
        it[h] = i_ref[h].T
    for one in exchange:
        one.wait_recv()
    z_own(anc)
    rs_arrived(p0)
    product_done(0)
    ag_round1(f0)
    rs_round2(p1, p_part(1), lambda k: ph.at[1, k])
    rs_arrived(p1)
    product_done(1)
    ag_round1(f1)
    z_relay(anc, 1)
    ag_round2(f0)
    z_relay(anc, 2)
    z_relay(0, 1)
    ag_arrived(f0)
    z_relay(anc, 3)
    z_last(anc)
    ancestor_times(0)
    ag_round1(q0)
    ag_round2(f1)
    ag_arrived(f1)
    ancestor_times(1)
    ag_round1(q1)
    ag_round2(q0)
    z_relay(0, 2)
    z_own(1)
    ag_arrived(q0)
    right_terms(0)
    ag_round2(q1)
    z_relay(0, 3)
    z_last(0)
    diagonal_partial(0)
    rs_round1(d0)
    z_relay(1, 1)
    ag_arrived(q1)
    right_terms(1)
    rs_round2(d0, d_part(0), lambda k: dh.at[0, k])
    z_relay(1, 2)
    z_relay(1, 3)
    z_last(1)
    diagonal_partial(1)
    rs_round1(d1)
    rs_arrived(d0)
    diagonal_done(0)
    rs_round2(d1, d_part(1), lambda k: dh.at[1, k])
    rs_arrived(d1)
    diagonal_done(1)

    for copies in (p0, p1, f0, f1, q0, q1, d0, d1, exchange):
        sent(copies)
    for item in range(group + 1):
        z_sent(item)


def body(sigma_root, structure, inv_diag, panel):
    leaves, rows, cols = lax.axis_size("leaf"), lax.axis_size("row"), lax.axis_size("col")
    group, kb, cb = inv_diag.shape
    ns = panel.shape[1]
    children = structure.shape[0]
    root_rows, root_cols = sigma_root.shape
    ra = ns // (rows * cols)
    sa = ns // leaves
    tb = ns // rows
    grid_pos = lax.axis_index("row") * cols + lax.axis_index("col")
    own_cols = lax.dynamic_slice_in_dim(structure, grid_pos * ra, ra, 1) - grid_pos * root_cols
    pick = (own_cols[:, :, None] == jnp.arange(root_cols, dtype=jnp.int32)[None, None, :]).astype(BF16)
    pick = pick.reshape(children * ra, root_cols)
    dma = pltpu.SemaphoreType.DMA
    vmem = pltpu.VMEM
    items = group + 1
    depth = cols // 2
    return pl.pallas_call(
        partial(kernel, (leaves, rows, cols, group, ns, kb, cb, root_rows)),
        out_shape=(
            jax.ShapeDtypeStruct((group, tb, cb), F32),
            jax.ShapeDtypeStruct((group, kb, cb), F32),
        ),
        in_specs=[pl.BlockSpec(memory_space=vmem)] * 5,
        out_specs=[pl.BlockSpec(memory_space=vmem)] * 2,
        scratch_shapes=[
            vmem((cols, group, kb, cb), F32),
            vmem((group, tb, ns), F32),
            vmem((children, ra, sa), F32),
            vmem((children * ra, root_rows), F32),
            vmem((group, ns, cb), F32),
            vmem((group, 2, tb // 2, cb), F32),
            vmem((group, 2, 2, tb // 2, cb), F32),
            vmem((group, ns, cb), F32),
            vmem((group, rows, cb, tb), F32),
            vmem((group, cb, kb), F32),
            vmem((group, cb, kb), F32),
            vmem((group, cols, cb, cb), F32),
            vmem((group, 2, cb, cb), F32),
            vmem((group, 2, 2, cb, cb), F32),
            dma((items, 2, depth - 1)), dma((items, 2, depth - 1)),
            dma((items, depth)), dma((items, depth)),
            dma((leaves - 1,)), dma((leaves - 1,)),
            dma((group, 6)), dma((group, 6)),
            dma((group, 6)), dma((group, 6)),
            dma((group, 6)), dma((group, 6)),
            dma((group, 6)), dma((group, 6)),
        ],
        compiler_params=pltpu.CompilerParams(
            collective_id=0, has_side_effects=True, vmem_limit_bytes=56 * 1024 * 1024
        ),
    )(panel, inv_diag, sigma_root, structure[:, None, :], pick)


def solution(mesh):
    placed = (P("leaf", ("row", "col")), P(), P("leaf", "row", "col"), P("leaf", None, "row"))
    return jax.shard_map(
        body,
        mesh=mesh,
        in_specs=placed,
        out_specs=(P("leaf", "row", "col"), P("leaf", "row", "col")),
        check_vma=False,
    )
```

time: 287 us -> 146 us (0.51)
  waiting for transfers between devices: 213 us -> 0 us
  Pallas kernels: 0 us -> 135 us
  matrix products: 36.9 us -> 0 us
  between operations: 15.3 us -> 0.65 us
  blocking collectives: 12.8 us -> 0 us
    pallas_call x0 -> x1, Pallas kernels: none -> 135 us  [body(): pl.pallas_call(partial(kernel, (leaves, rows, cols, group, ns, kb, cb, ro...]
    all_gather x3 -> x0, waiting for transfers between devices: 119 us -> none  [the longest x1 86.5 us: body(): gathered = lax.all_gather(inv_diag, 'col', axis=2, tiled=True)]
    reduce_scatter x1 -> x0, waiting for transfers between devices: 48.5 us -> none  [body(): lax.psum_scatter(partials, 'row', scatter_dimension=1, tiled=True)]
    psum x1 -> x0, waiting for transfers between devices: 45 us -> none  [body(): product = lax.psum(mm('msk,mkj->msj', panel, inv_diag), 'row')]
    dot_general x6 -> x0, matrix products: 36.9 us -> none  [mm(): jnp.einsum(spec, a, b, precision=HIGHEST, preferred_element_type=jnp.floa...]
    all_to_all x1 -> x0, blocking collectives: 12.8 us -> none  [body(): got = lax.all_to_all(picked, 'leaf', 0, 0)]
  transfers between devices with their start and end apart: 5 -> 0, of which waited for: 4 -> 0; matrix products, arithmetic and copies ran while one was open for 6% -> 0% of each run, Pallas kernels for 0% -> 0%
where the time goes in v2:
time: 146 us; the launch traced here: 143 us
  Pallas kernels  135 us (92%)
  local copies, waits for them, and re-layouts  5.73 us (4%)
  other arithmetic  1.61 us (1%)
    pallas_call x1, Pallas kernels, body(): pl.pallas_call(partial(kernel, (leaves, rows, cols, group, ns, kb, cb, ro...  135 us
    unnamed x2, local copies, waits for them, and re-layouts  4.13 us

profile of v2, /device:TPU:231, one launch (start us, length us, event | category | flops | bytes accessed | tf_op | source)
XLA Modules:
  0.0 143.5 jit_solution(5332595210055086281)
XLA Ops:
  0.6 0.8 dynamic-slice_subtract_fusion
  1.4 0.1 eq.16
  1.5 1.5 %broadcast_in_dim.2.st_ref = s32[16,1,1024]{2,1,0:T(1,128)} reshape(s32[16,1024]{1,0:T(8,128)} %param.5) | data formatting | bytes 131072 | tf_op jit(solution)/shard_map/broadcast_in_dim | solution.py:415
  3.0 0.8 fusion.pick_ref
  3.8 135.5 %shard_map.59 = (f32[2,256,256]{2,1,0:T(8,128)}, f32[2,512,256]{2,1,0:T(8,128)}) custom-call(f32[2,1024,512]{2,1,0:T(8,128)} %w_ref.1, f32[2,512,256]{2,1,0:T(8,128)} %i_ref.1, f32[1024,256]{1,0:T(8,128)} %sig_ref.1, s32[16,1,1024]{2,1,0:T(1,128)} %broadcast_in_dim.2.st_ref, bf16[512,256]{1,0:T(8,128)(2,1)} %fusion.pick_ref), custom_call_target="tpu_custom_call" | custom-call | tf_op jit(solution)/shard_map/pallas_call | solution.py:381
  139.3 1.9 %copy.8 = f32[2,256,256]{2,1,0:T(8,128)} copy(f32[2,256,256]{2,1,0:T(8,128)} %get-tuple-element.4) | data formatting | bytes 1048576
  141.2 2.3 %copy.9 = f32[2,512,256]{2,1,0:T(8,128)} copy(f32[2,512,256]{2,1,0:T(8,128)} %get-tuple-element.5) | data formatting | bytes 2097152

commit v3 on v2

--- a/solution.py
+++ b/solution.py
@@ -43,7 +43,7 @@
     w_ref, i_ref, sig_ref, st_ref, pick_ref,
     sp_ref, sd_ref,
     ig, aa, asend, yt, pp, ph, pr, pf, qt, it, nt, dp, dh, dr,
-    z_ss, z_rs, b_ss, b_rs, l_ss, l_rs, p_ss, p_rs, a_ss, a_rs, s_ss, s_rs, d_ss, d_rs,
+    ml, z_ss, z_rs, b_ss, b_rs, l_ss, l_rs, p_ss, p_rs, a_ss, a_rs, s_ss, s_rs, d_ss, d_rs, m_ss, m_rs,
 ):
     leaves, rows, cols, group, ns, kb, cb, root_rows = sizes
     depth = cols // 2
@@ -77,6 +77,15 @@
     def _():
         pl.semaphore_signal(barrier, inc=1, device_id={"col": c + 2}, device_id_type=MESH)
 
+    corner = jnp.logical_or(
+        jnp.logical_and(y == 0, z == depth - 1), jnp.logical_and(y == rows - 1, z == 0)
+    )
+
+    @pl.when(corner)
+    def _():
+        for k in range(2):
+            pl.semaphore_signal(barrier, inc=1, device_id={"row": z, "col": 2 * y + k}, device_id_type=MESH)
+
     def view(item, slot):
         if item < group:
             return ig.at[slot, item]
@@ -90,32 +99,52 @@
             z_ss.at[item, way, step - 1], z_rs.at[item, way, step - 1], {"col": target},
         )
 
-    def z_sends(way, step):
+    def z_cut(item, way, step):
+        return step == depth - 1 and ((item == 0 and way == 1) or (item == 1 and way == 0))
+
+    def z_sends(item, way, step):
+        if z_cut(item, way, step):
+            return None
         if way == 0:
-            return jnp.logical_and(z < depth - 1, z >= step - 1)
-        return jnp.logical_and(z > 0, z + step - 1 <= depth - 1)
-
-    def z_gets(way, step):
-        return z >= step if way == 0 else z + step <= depth - 1
+            cond, origin = jnp.logical_and(z < depth - 1, z >= step - 1), z - step + 1
+        else:
+            cond, origin = jnp.logical_and(z > 0, z + step - 1 <= depth - 1), z + step - 1
+        return jnp.logical_and(cond, origin <= y) if item < group else cond
+
+    def z_gets(item, way, step):
+        if z_cut(item, way, step):
+            return None
+        cond, origin = (z >= step, z - step) if way == 0 else (z + step <= depth - 1, z + step)
+        return jnp.logical_and(cond, origin <= y) if item < group else cond
+
+    def when(cond, do):
+        if cond is not None:
+            pl.when(cond)(do)
+
+    def has_own(item):
+        return z <= y if item < group else z >= 0
 
     def b_copy(item, origin):
         slot = 2 * origin + core
         return copy(view(item, slot), view(item, slot), b_ss.at[item, origin], b_rs.at[item, origin], {"col": sibling})
 
+    def b_landed(item, origin):
+        slot = 2 * origin + 1 - core
+        copy(
+            view(item, slot), view(item, slot), b_ss.at[item, origin], b_rs.at[item, origin], {"col": sibling}
+        ).wait_recv()
+
     def z_start(item, way, step):
-        @pl.when(z_sends(way, step))
-        def _():
-            z_copy(item, way, step).start()
+        when(z_sends(item, way, step), lambda: z_copy(item, way, step).start())
 
     def z_own(item):
         z_start(item, 0, 1)
         z_start(item, 1, 1)
-        b_copy(item, z).start()
+        when(has_own(item), lambda: b_copy(item, z).start())
 
     def z_relay(item, step):
         for way in range(2):
-            @pl.when(z_gets(way, step))
-            def _():
+            def relay():
                 origin = z - step if way == 0 else z + step
                 slot = 2 * origin + core
                 copy(
@@ -126,21 +155,18 @@
                     z_start(item, way, step + 1)
                 b_copy(item, origin).start()
 
+            when(z_gets(item, way, step), relay)
+
     def z_last(item):
         for origin in range(depth):
-            slot = 2 * origin + 1 - core
-            copy(
-                view(item, slot), view(item, slot), b_ss.at[item, origin], b_rs.at[item, origin], {"col": sibling}
-            ).wait_recv()
+            b_landed(item, origin)
 
     def z_sent(item):
         for way in range(2):
             for step in range(1, depth):
-                @pl.when(z_sends(way, step))
-                def _():
-                    z_copy(item, way, step).wait_send()
-        for origin in range(depth):
-            b_copy(item, origin).wait_send()
+                when(z_sends(item, way, step), lambda: z_copy(item, way, step).wait_send())
+                when(z_gets(item, way, step), lambda: b_copy(item, z - step if way == 0 else z + step).wait_send())
+        when(has_own(item), lambda: b_copy(item, z).wait_send())
 
     def rs_copies(part, half, whole, ss, rs):
         right, left = {"row": y_next}, {"row": y_prev}
@@ -273,19 +299,124 @@
         def _(s):
             nt[h] = nt[h] + dot3(qt[h, s], w_ref[h, pl.ds(pl.multiple_of(s * tb, tb), tb), :])
 
-    def diagonal_partial(h):
-        @pl.loop(0, cols)
-        def _(slot):
-            dp[h, slot] = dot3(nt[h], ig[slot, h])
-
-    def diagonal_done(h):
+    def uncut(h):
+        return z < depth - 1 if h == 1 else z >= 0
+
+    def d_goes(h):
+        late = jnp.logical_or(y >= 2, jnp.logical_and(y == 1, uncut(h)))
+        far = jnp.logical_or(y == 3, jnp.logical_and(y == 2, uncut(h)))
+        wrap = jnp.logical_and(y == 3, uncut(h))
+        return (far, far, wrap, late, jnp.logical_or(y == 0, wrap), late)
+
+    def diagonal_slice(h, copies, origin):
+        b_landed(h, origin)
         for k in range(2):
-            total = dp[h, 2 * y + k] + (dr[h, 0, k] + dr[h, 1, k])
-            sd_ref[h, pl.ds(k * cb, cb), :] = total.T
+            dp[h, 2 * origin + k] = dot3(nt[h], ig[2 * origin + k, h])
+
+        @pl.when(origin == y_far)
+        def _():
+            copies[0].start()
+            copies[1].start()
+
+        @pl.when(origin == y_next)
+        def _():
+            copies[2].start()
+
+        @pl.when(origin == y_prev)
+        def _():
+            copies[3].start()
+
+            @pl.when(y == 3)
+            def _():
+                copies[5].start()
+
+    def diagonal_step(h, copies, step):
+        if step == 0:
+            when(z <= y, lambda: diagonal_slice(h, copies, z))
+            return
+        for way in range(2):
+            when(z_gets(h, way, step), lambda: diagonal_slice(h, copies, z - step if way == 0 else z + step))
+
+    def d_round2(h, copies):
+        @pl.when(jnp.logical_and(y == 3, uncut(h)))
+        def _():
+            copies[0].wait_recv()
+            dp[h, 0] = dp[h, 0] + dh[h, 0]
+            copies[4].start()
+
+        @pl.when(y == 0)
+        def _():
+            copies[0].wait_recv()
+            dp[h, 2] = dh[h, 0]
+            copies[4].start()
+
+        @pl.when(jnp.logical_or(y == 2, jnp.logical_and(y == 1, uncut(h))))
+        def _():
+            copies[1].wait_recv()
+            mine = d_part(h)(y_prev, 1)
+            mine[...] = mine[...] + dh[h, 1]
+            copies[5].start()
+
+    def d_finish(h, copies):
+        first = jnp.logical_and(y == 0, uncut(h))
+        middle = jnp.logical_or(y == 1, y == 2)
+
+        @pl.when(jnp.logical_or(first, middle))
+        def _():
+            copies[3].wait_recv()
+            dp[h, 2 * y] = dp[h, 2 * y] + dr[h, 1, 0]
+
+        @pl.when(jnp.logical_or(first, y == 1))
+        def _():
+            copies[4].wait_recv()
+            dp[h, 2 * y] = dp[h, 2 * y] + dr[h, 0, 0]
+
+        @pl.when(first)
+        def _():
+            copies[2].wait_recv()
+            dp[h, 2 * y + 1] = dp[h, 2 * y + 1] + dr[h, 0, 1]
+
+        @pl.when(jnp.logical_or(first, middle))
+        def _():
+            copies[5].wait_recv()
+            dp[h, 2 * y + 1] = dp[h, 2 * y + 1] + dr[h, 1, 1]
+
+        mirrored = jnp.logical_and(corner, (y == 3) if h == 0 else (y == 0))
+
+        @pl.when(jnp.logical_not(mirrored))
+        def _():
+            for k in range(2):
+                sd_ref[h, pl.ds(k * cb, cb), :] = dp[h, 2 * y + k].T
+
+    def m_copy(h, k):
+        return copy(dp.at[h, 2 * y + k], ml.at[core], m_ss.at[k], m_rs.at[core], {"row": z, "col": 2 * y + k})
+
+    def m_sends(h):
+        return jnp.logical_and(corner, (y == 0) if h == 0 else (y == 3))
+
+    def m_start(h):
+        @pl.when(m_sends(h))
+        def _():
+            for k in range(2):
+                m_copy(h, k).start()
+
+    def m_finish(h):
+        @pl.when(jnp.logical_and(corner, (y == 3) if h == 0 else (y == 0)))
+        def _():
+            for k in range(2):
+                copy(ml.at[k], ml.at[k], m_ss.at[k], m_rs.at[k], {"row": z}).wait_recv()
+                sd_ref[h, pl.ds(k * cb, cb), :] = ml[k]
+
+        @pl.when(m_sends(h))
+        def _():
+            for k in range(2):
+                m_copy(h, k).wait_send()
 
     ig[c] = i_ref[...]
     product_partial(0)
-    pl.semaphore_wait(barrier, 2 + leaves + (z > 0).astype(jnp.int32) + (z < depth - 1).astype(jnp.int32))
+    pick()
+    pl.semaphore_wait(barrier, 2 + leaves + (z > 0).astype(jnp.int32) + (z < depth - 1).astype(jnp.int32)
+        + 2 * corner.astype(jnp.int32))
 
     anc = group
     p0, p1 = p_rs_copies(0), p_rs_copies(1)
@@ -295,68 +426,74 @@
     exchange = l_copies()
 
     rs_round1(p0)
-    z_own(0)
-    pick()
     for one in exchange:
         one.start()
     aa[:, pl.ds(pl.multiple_of(c * ra, ra), ra), pl.ds(pl.multiple_of(leaf * sa, sa), sa)] = asend[
         pl.ds(leaf * group, group)
     ]
+    z_own(0)
+    rs_round2(p0, p_part(0), lambda k: ph.at[0, k])
+    rs_arrived(p0)
+    product_done(0)
+    ag_round1(f0)
     product_partial(1)
     rs_round1(p1)
-    rs_round2(p0, p_part(0), lambda k: ph.at[0, k])
-    for h in range(group):
-        it[h] = i_ref[h].T
     for one in exchange:
         one.wait_recv()
     z_own(anc)
-    rs_arrived(p0)
-    product_done(0)
-    ag_round1(f0)
+    ag_round2(f0)
+    z_relay(anc, 1)
     rs_round2(p1, p_part(1), lambda k: ph.at[1, k])
     rs_arrived(p1)
     product_done(1)
     ag_round1(f1)
-    z_relay(anc, 1)
-    ag_round2(f0)
     z_relay(anc, 2)
-    z_relay(0, 1)
+    ag_round2(f1)
+    z_relay(anc, 3)
     ag_arrived(f0)
-    z_relay(anc, 3)
     z_last(anc)
     ancestor_times(0)
     ag_round1(q0)
-    ag_round2(f1)
+    z_relay(0, 1)
+    ag_round2(q0)
+    for h in range(group):
+        it[h] = i_ref[h].T
     ag_arrived(f1)
     ancestor_times(1)
     ag_round1(q1)
-    ag_round2(q0)
     z_relay(0, 2)
-    z_own(1)
     ag_arrived(q0)
     right_terms(0)
+    z_own(1)
     ag_round2(q1)
+    diagonal_step(0, d0, 0)
+    diagonal_step(0, d0, 1)
     z_relay(0, 3)
-    z_last(0)
-    diagonal_partial(0)
-    rs_round1(d0)
-    z_relay(1, 1)
+    diagonal_step(0, d0, 2)
+    diagonal_step(0, d0, 3)
     ag_arrived(q1)
     right_terms(1)
-    rs_round2(d0, d_part(0), lambda k: dh.at[0, k])
+    z_relay(1, 1)
+    diagonal_step(1, d1, 0)
+    diagonal_step(1, d1, 1)
+    d_round2(0, d0)
     z_relay(1, 2)
+    diagonal_step(1, d1, 2)
+    d_finish(0, d0)
+    m_start(0)
     z_relay(1, 3)
-    z_last(1)
-    diagonal_partial(1)
-    rs_round1(d1)
-    rs_arrived(d0)
-    diagonal_done(0)
-    rs_round2(d1, d_part(1), lambda k: dh.at[1, k])
-    rs_arrived(d1)
-    diagonal_done(1)
-
-    for copies in (p0, p1, f0, f1, q0, q1, d0, d1, exchange):
+    diagonal_step(1, d1, 3)
+    m_start(1)
+    d_round2(1, d1)
+    d_finish(1, d1)
+    m_finish(0)
+    m_finish(1)
+
+    for copies in (p0, p1, f0, f1, q0, q1, exchange):
         sent(copies)
+    for h, copies in enumerate((d0, d1)):
+        for cond, one in zip(d_goes(h), copies):
+            when(cond, one.wait_send)
     for item in range(group + 1):
         z_sent(item)
 
@@ -401,6 +538,7 @@
             vmem((group, cols, cb, cb), F32),
             vmem((group, 2, cb, cb), F32),
             vmem((group, 2, 2, cb, cb), F32),
+            vmem((2, cb, cb), F32),
             dma((items, 2, depth - 1)), dma((items, 2, depth - 1)),
             dma((items, depth)), dma((items, depth)),
             dma((leaves - 1,)), dma((leaves - 1,)),
@@ -408,6 +546,7 @@
             dma((group, 6)), dma((group, 6)),
             dma((group, 6)), dma((group, 6)),
             dma((group, 6)), dma((group, 6)),
+            dma((2,)), dma((2,)),
         ],
         compiler_params=pltpu.CompilerParams(
             collective_id=0, has_side_effects=True, vmem_limit_bytes=56 * 1024 * 1024

time: 146 us -> 131 us (0.90)
  Pallas kernels: 135 us -> 122 us
    pallas_call x1, Pallas kernels: 135 us -> 122 us  [body(): pl.pallas_call(partial(kernel, (leaves, rows, cols, group, ns, kb, cb, ro...]
where the time goes in v3:
time: 131 us; the launch traced here: 130 us
  Pallas kernels  122 us (93%)
  local copies, waits for them, and re-layouts  5.73 us (4%)
  other arithmetic  1.61 us (1%)
    pallas_call x1, Pallas kernels, body(): pl.pallas_call(partial(kernel, (leaves, rows, cols, group, ns, kb, cb, ro...  122 us
    unnamed x2, local copies, waits for them, and re-layouts  4.13 us

profile of v3, /device:TPU:231, one launch (start us, length us, event | category | flops | bytes accessed | tf_op | source)
XLA Modules:
  0.0 129.9 jit_solution(3121297771466927937)
XLA Ops:
  0.6 0.8 dynamic-slice_subtract_fusion
  1.4 0.1 eq.16
  1.5 1.5 %broadcast_in_dim.2.st_ref = s32[16,1,1024]{2,1,0:T(1,128)} reshape(s32[16,1024]{1,0:T(8,128)} %param.5) | data formatting | bytes 131072 | tf_op jit(solution)/shard_map/broadcast_in_dim | solution.py:554
  3.0 0.8 fusion.pick_ref
  3.8 121.9 %shard_map.59 = (f32[2,256,256]{2,1,0:T(8,128)}, f32[2,512,256]{2,1,0:T(8,128)}) custom-call(f32[2,1024,512]{2,1,0:T(8,128)} %w_ref.1, f32[2,512,256]{2,1,0:T(8,128)} %i_ref.1, f32[1024,256]{1,0:T(8,128)} %sig_ref.1, s32[16,1,1024]{2,1,0:T(1,128)} %broadcast_in_dim.2.st_ref, bf16[512,256]{1,0:T(8,128)(2,1)} %fusion.pick_ref), custom_call_target="tpu_custom_call" | custom-call | tf_op jit(solution)/shard_map/pallas_call | solution.py:518
  125.8 1.9 %copy.8 = f32[2,256,256]{2,1,0:T(8,128)} copy(f32[2,256,256]{2,1,0:T(8,128)} %get-tuple-element.4) | data formatting | bytes 1048576
  127.6 2.3 %copy.9 = f32[2,512,256]{2,1,0:T(8,128)} copy(f32[2,512,256]{2,1,0:T(8,128)} %get-tuple-element.5) | data formatting | bytes 2097152

commit v4 on v3

--- a/solution.py
+++ b/solution.py
@@ -17,13 +17,6 @@
     return high, (x - high.astype(F32)).astype(BF16)
 
 
-def split3(x):
-    high = x.astype(BF16)
-    rest = x - high.astype(F32)
-    mid = rest.astype(BF16)
-    return high, mid, (rest - mid.astype(F32)).astype(BF16)
-
-
 def dot(a, b):
     return lax.dot_general(a, b, (((1,), (0,)), ((), ())), preferred_element_type=F32)
 
@@ -40,12 +33,12 @@
 
 def kernel(
     sizes,
-    w_ref, i_ref, sig_ref, st_ref, pick_ref,
+    w_hbm, i_ref, sig_hbm, st_ref,
     sp_ref, sd_ref,
-    ig, aa, asend, yt, pp, ph, pr, pf, qt, it, nt, dp, dh, dr,
-    ml, z_ss, z_rs, b_ss, b_rs, l_ss, l_rs, p_ss, p_rs, a_ss, a_rs, s_ss, s_rs, d_ss, d_rs, m_ss, m_rs,
+    w_ref, sig_ref, ig, aa, asend, hot_col, col_idx, row_idx, yt, pp, ph, pr, pf, qt, it, nt, dp, dh, dr,
+    ml, z_ss, z_rs, b_ss, b_rs, l_ss, l_rs, p_ss, p_rs, a_ss, a_rs, s_ss, s_rs, d_ss, d_rs, m_ss, m_rs, in_sem,
 ):
-    leaves, rows, cols, group, ns, kb, cb, root_rows = sizes
+    leaves, rows, cols, group, ns, kb, cb, root_rows, root_cols = sizes
     depth = cols // 2
     tb = ns // rows
     ra = ns // (rows * cols)
@@ -63,6 +56,12 @@
             src_ref=src, dst_ref=dst, send_sem=ss, recv_sem=rs, device_id=target, device_id_type=MESH
         )
 
+    fetch = [pltpu.make_async_copy(w_hbm.at[h], w_ref.at[h], in_sem.at[h]) for h in range(group)]
+    fetch_root = pltpu.make_async_copy(sig_hbm, sig_ref, in_sem.at[group])
+    fetch[0].start()
+    fetch_root.start()
+    fetch[1].start()
+
     barrier = pltpu.get_barrier_semaphore()
     for target in ({"row": y_next}, {"row": y_prev}, {"col": sibling}):
         pl.semaphore_signal(barrier, inc=1, device_id=target, device_id_type=MESH)
@@ -89,7 +88,7 @@
     def view(item, slot):
         if item < group:
             return ig.at[slot, item]
-        return aa.at[:, pl.ds(pl.multiple_of(slot * ra, ra), ra), :]
+        return aa.at[item - group, pl.ds(pl.multiple_of(slot * ra, ra), ra), :]
 
     def z_copy(item, way, step):
         slot = c - 2 * (step - 1) if way == 0 else c + 2 * (step - 1)
@@ -251,23 +250,36 @@
             copies[k].wait_recv()
 
     def product_partial(h):
+        fetch[h].wait()
+
         @pl.loop(0, rows)
         def _(s):
             at = pl.ds(pl.multiple_of(s * tb, tb), tb)
             pp[h, at, :] = dot3(w_ref[h, at, :], i_ref[h])
 
     def pick():
-        sig_parts = split3(sig_ref[...])
-        chosen = pick_ref[...]
-        yt[...] = dot_t(chosen, sig_parts[0]) + (dot_t(chosen, sig_parts[1]) + dot_t(chosen, sig_parts[2]))
+        fetch_root.wait()
+        place = y * cols + c
+        share = pl.multiple_of((place * ra) // 128 * 128, 128)
+        col_idx[...] = st_ref[:, pl.ds(share, min(128, ns))].T - place * root_cols
+        mine = col_idx[pl.ds(pl.multiple_of(place * ra - share, ra), ra), :]
         at = pl.ds(pl.multiple_of(leaf * sa, sa), sa)
+        lanes = lax.broadcasted_iota(jnp.int32, (ra, root_cols), 1)
+        for h in range(leaves * group):
+            row_idx[h] = st_ref[pl.ds(h, 1), at] - leaf * root_rows
+            hot_col[pl.ds(h * ra, ra), :] = jnp.where(lanes == mine[:, h : h + 1], 1.0, 0.0).astype(BF16)
+        high, low = split(sig_ref[...])
+        chosen = hot_col[...]
+        yt[0] = dot_t(chosen, high).astype(BF16)
+        yt[1] = dot_t(chosen, low).astype(BF16)
+        sublanes = lax.broadcasted_iota(jnp.int32, (root_rows, sa), 0)
 
         @pl.loop(0, leaves * group)
         def _(h):
-            local = st_ref[h, :, at] - leaf * root_rows
-            hot = jnp.where(lax.broadcasted_iota(jnp.int32, (root_rows, sa), 0) == local, 1.0, 0.0).astype(BF16)
-            parts = split3(yt[pl.ds(pl.multiple_of(h * ra, ra), ra), :])
-            asend[h] = dot(parts[0], hot) + (dot(parts[1], hot) + dot(parts[2], hot))
+            hot = jnp.where(sublanes == row_idx[h], 1.0, 0.0).astype(BF16)
+            mine = pl.ds(pl.multiple_of(h * ra, ra), ra)
+            both = dot(jnp.concatenate([yt[0, mine, :], yt[1, mine, :]], axis=0), hot)
+            asend[h] = both[:ra] + both[ra:]
 
     def l_copies():
         out = []
@@ -412,25 +424,23 @@
             for k in range(2):
                 m_copy(h, k).wait_send()
 
+    p0, p1 = p_rs_copies(0), p_rs_copies(1)
+    f0, f1 = pf_copies(0), pf_copies(1)
+    q0, q1 = qt_copies(0), qt_copies(1)
+    d0, d1 = d_rs_copies(0), d_rs_copies(1)
+    exchange = l_copies()
+
     ig[c] = i_ref[...]
     product_partial(0)
     pick()
     pl.semaphore_wait(barrier, 2 + leaves + (z > 0).astype(jnp.int32) + (z < depth - 1).astype(jnp.int32)
         + 2 * corner.astype(jnp.int32))
-
-    anc = group
-    p0, p1 = p_rs_copies(0), p_rs_copies(1)
-    f0, f1 = pf_copies(0), pf_copies(1)
-    q0, q1 = qt_copies(0), qt_copies(1)
-    d0, d1 = d_rs_copies(0), d_rs_copies(1)
-    exchange = l_copies()
-
-    rs_round1(p0)
     for one in exchange:
         one.start()
     aa[:, pl.ds(pl.multiple_of(c * ra, ra), ra), pl.ds(pl.multiple_of(leaf * sa, sa), sa)] = asend[
         pl.ds(leaf * group, group)
     ]
+    rs_round1(p0)
     z_own(0)
     rs_round2(p0, p_part(0), lambda k: ph.at[0, k])
     rs_arrived(p0)
@@ -440,25 +450,30 @@
     rs_round1(p1)
     for one in exchange:
         one.wait_recv()
-    z_own(anc)
+    z_own(2)
+    z_own(3)
     ag_round2(f0)
-    z_relay(anc, 1)
+    z_relay(2, 1)
+    z_relay(2, 2)
     rs_round2(p1, p_part(1), lambda k: ph.at[1, k])
     rs_arrived(p1)
     product_done(1)
     ag_round1(f1)
-    z_relay(anc, 2)
-    ag_round2(f1)
-    z_relay(anc, 3)
+    z_relay(3, 1)
+    z_relay(2, 3)
     ag_arrived(f0)
-    z_last(anc)
+    z_last(2)
     ancestor_times(0)
     ag_round1(q0)
     z_relay(0, 1)
+    ag_round2(f1)
+    z_relay(3, 2)
     ag_round2(q0)
     for h in range(group):
         it[h] = i_ref[h].T
+    z_relay(3, 3)
     ag_arrived(f1)
+    z_last(3)
     ancestor_times(1)
     ag_round1(q1)
     z_relay(0, 2)
@@ -494,8 +509,13 @@
     for h, copies in enumerate((d0, d1)):
         for cond, one in zip(d_goes(h), copies):
             when(cond, one.wait_send)
-    for item in range(group + 1):
+    for item in range(2 * group):
         z_sent(item)
+
+
+def hand_over(sp_in, sd_in, sp_out, sd_out):
+    sp_out[...] = sp_in[...]
+    sd_out[...] = sd_in[...]
 
 
 def body(sigma_root, structure, inv_diag, panel):
@@ -507,27 +527,28 @@
     ra = ns // (rows * cols)
     sa = ns // leaves
     tb = ns // rows
-    grid_pos = lax.axis_index("row") * cols + lax.axis_index("col")
-    own_cols = lax.dynamic_slice_in_dim(structure, grid_pos * ra, ra, 1) - grid_pos * root_cols
-    pick = (own_cols[:, :, None] == jnp.arange(root_cols, dtype=jnp.int32)[None, None, :]).astype(BF16)
-    pick = pick.reshape(children * ra, root_cols)
     dma = pltpu.SemaphoreType.DMA
     vmem = pltpu.VMEM
-    items = group + 1
+    items = 2 * group
     depth = cols // 2
-    return pl.pallas_call(
-        partial(kernel, (leaves, rows, cols, group, ns, kb, cb, root_rows)),
+    made = pl.pallas_call(
+        partial(kernel, (leaves, rows, cols, group, ns, kb, cb, root_rows, root_cols)),
         out_shape=(
             jax.ShapeDtypeStruct((group, tb, cb), F32),
             jax.ShapeDtypeStruct((group, kb, cb), F32),
         ),
-        in_specs=[pl.BlockSpec(memory_space=vmem)] * 5,
+        in_specs=[pl.BlockSpec(memory_space=kind) for kind in (pl.ANY, vmem, pl.ANY, vmem)],
         out_specs=[pl.BlockSpec(memory_space=vmem)] * 2,
         scratch_shapes=[
+            vmem(panel.shape, F32),
+            vmem(sigma_root.shape, F32),
             vmem((cols, group, kb, cb), F32),
             vmem((group, tb, ns), F32),
             vmem((children, ra, sa), F32),
-            vmem((children * ra, root_rows), F32),
+            vmem((children * ra, root_cols), BF16),
+            vmem((min(128, ns), children), jnp.int32),
+            vmem((children, 1, sa), jnp.int32),
+            vmem((2, children * ra, root_rows), BF16),
             vmem((group, ns, cb), F32),
             vmem((group, 2, tb // 2, cb), F32),
             vmem((group, 2, 2, tb // 2, cb), F32),
@@ -547,11 +568,15 @@
             dma((group, 6)), dma((group, 6)),
             dma((group, 6)), dma((group, 6)),
             dma((2,)), dma((2,)),
+            dma((group + 1,)),
         ],
         compiler_params=pltpu.CompilerParams(
             collective_id=0, has_side_effects=True, vmem_limit_bytes=56 * 1024 * 1024
         ),
-    )(panel, inv_diag, sigma_root, structure[:, None, :], pick)
+    )(panel, inv_diag, sigma_root, structure)
+    return pl.pallas_call(
+        hand_over, out_shape=tuple(jax.ShapeDtypeStruct(one.shape, one.dtype) for one in made)
+    )(*made)
 
 
 def solution(mesh):

time: 131 us -> 125 us (0.954)
  local copies, waits for them, and re-layouts: 5.73 us -> 0 us
  other arithmetic: 1.61 us -> 0 us
    unnamed x2 -> x0, local copies, waits for them, and re-layouts: 4.13 us -> none
    pallas_call x0 -> x1, Pallas kernels: none -> 2.57 us  [body(): pl.pallas_call(hand_over, out_shape=tuple((jax.ShapeDtypeStruct(one.shape...]
    broadcast_in_dim x1 -> x0, local copies, waits for them, and re-layouts: 1.52 us -> none  [body(): structure[:, None, :]]
where the time goes in v4:
time: 125 us; the launch traced here: 124 us
  Pallas kernels  123 us (98%)
    pallas_call x1, Pallas kernels, body(): pl.pallas_call(partial(kernel, (leaves, rows, cols, group, ns, kb, cb, ro...  121 us
    pallas_call x1, Pallas kernels, body(): pl.pallas_call(hand_over, out_shape=tuple((jax.ShapeDtypeStruct(one.shape...  2.57 us

profile of v4, /device:TPU:231, one launch (start us, length us, event | category | flops | bytes accessed | tf_op | source)
XLA Modules:
  0.0 124.0 jit_solution(7836634965938942746)
XLA Ops:
  0.6 120.7 %shard_map.59 = (f32[2,256,256]{2,1,0:T(8,128)}, f32[2,512,256]{2,1,0:T(8,128)}) custom-call(f32[2,1024,512]{2,1,0:T(8,128)} %w_hbm.1, f32[2,512,256]{2,1,0:T(8,128)} %i_ref.1, f32[1024,256]{1,0:T(8,128)} %sig_hbm.1, s32[16,1024]{1,0:T(8,128)} %st_ref.1), custom_call_target="tpu_custom_call" | custom-call | tf_op jit(solution)/shard_map/pallas_call | solution.py:534
  121.4 2.6 %shard_map.60 = (f32[2,256,256]{2,1,0:T(8,128)}, f32[2,512,256]{2,1,0:T(8,128)}) custom-call(f32[2,256,256]{2,1,0:T(8,128)} %get-tuple-element.4.sp_in, f32[2,512,256]{2,1,0:T(8,128)} %get-tuple-element.5.sd_in), custom_call_target="tpu_custom_call" | custom-call | tf_op jit(solution)/shard_map/pallas_call | solution.py:577

commit v5 on v4

--- a/solution.py
+++ b/solution.py
@@ -460,12 +460,12 @@
     product_done(1)
     ag_round1(f1)
     z_relay(3, 1)
+    z_relay(0, 1)
     z_relay(2, 3)
     ag_arrived(f0)
     z_last(2)
     ancestor_times(0)
     ag_round1(q0)
-    z_relay(0, 1)
     ag_round2(f1)
     z_relay(3, 2)
     ag_round2(q0)
@@ -477,9 +477,9 @@
     ancestor_times(1)
     ag_round1(q1)
     z_relay(0, 2)
+    z_own(1)
     ag_arrived(q0)
     right_terms(0)
-    z_own(1)
     ag_round2(q1)
     diagonal_step(0, d0, 0)
     diagonal_step(0, d0, 1)
@@ -488,10 +488,10 @@
     diagonal_step(0, d0, 3)
     ag_arrived(q1)
     right_terms(1)
+    diagonal_step(1, d1, 0)
+    d_round2(0, d0)
     z_relay(1, 1)
-    diagonal_step(1, d1, 0)
     diagonal_step(1, d1, 1)
-    d_round2(0, d0)
     z_relay(1, 2)
     diagonal_step(1, d1, 2)
     d_finish(0, d0)

time: 125 us -> 124 us (level)
    pallas_call x1, Pallas kernels: 121 us -> 119 us  [body(): pl.pallas_call(partial(kernel, (leaves, rows, cols, group, ns, kb, cb, ro...]
where the time goes in v5:
time: 124 us; the launch traced here: 122 us
  Pallas kernels  122 us (98%)
    pallas_call x1, Pallas kernels, body(): pl.pallas_call(partial(kernel, (leaves, rows, cols, group, ns, kb, cb, ro...  119 us
    pallas_call x1, Pallas kernels, body(): pl.pallas_call(hand_over, out_shape=tuple((jax.ShapeDtypeStruct(one.shape...  2.57 us

profile of v5, /device:TPU:231, one launch (start us, length us, event | category | flops | bytes accessed | tf_op | source)
XLA Modules:
  0.0 122.4 jit_solution(736443236290016168)
XLA Ops:
  0.6 119.2 %shard_map.59 = (f32[2,256,256]{2,1,0:T(8,128)}, f32[2,512,256]{2,1,0:T(8,128)}) custom-call(f32[2,1024,512]{2,1,0:T(8,128)} %w_hbm.1, f32[2,512,256]{2,1,0:T(8,128)} %i_ref.1, f32[1024,256]{1,0:T(8,128)} %sig_hbm.1, s32[16,1024]{1,0:T(8,128)} %st_ref.1), custom_call_target="tpu_custom_call" | custom-call | tf_op jit(solution)/shard_map/pallas_call | solution.py:534
  119.9 2.6 %shard_map.60 = (f32[2,256,256]{2,1,0:T(8,128)}, f32[2,512,256]{2,1,0:T(8,128)}) custom-call(f32[2,256,256]{2,1,0:T(8,128)} %get-tuple-element.4.sp_in, f32[2,512,256]{2,1,0:T(8,128)} %get-tuple-element.5.sd_in), custom_call_target="tpu_custom_call" | custom-call | tf_op jit(solution)/shard_map/pallas_call | solution.py:577

commit v6 on v5

--- a/solution.py
+++ b/solution.py
@@ -140,6 +140,14 @@
         z_start(item, 0, 1)
         z_start(item, 1, 1)
         when(has_own(item), lambda: b_copy(item, z).start())
+
+    def z_own_early(item):
+        when(jnp.logical_and(z_sends(item, 0, 1), z < depth - 2), lambda: z_copy(item, 0, 1).start())
+        z_start(item, 1, 1)
+        when(has_own(item), lambda: b_copy(item, z).start())
+
+    def z_own_late(item):
+        when(jnp.logical_and(z_sends(item, 0, 1), z == depth - 2), lambda: z_copy(item, 0, 1).start())
 
     def z_relay(item, step):
         for way in range(2):
@@ -468,6 +476,7 @@
     ag_round1(q0)
     ag_round2(f1)
     z_relay(3, 2)
+    z_own_early(1)
     ag_round2(q0)
     for h in range(group):
         it[h] = i_ref[h].T
@@ -477,7 +486,7 @@
     ancestor_times(1)
     ag_round1(q1)
     z_relay(0, 2)
-    z_own(1)
+    z_own_late(1)
     ag_arrived(q0)
     right_terms(0)
     ag_round2(q1)

time: 124 us -> 126 us (1.016)
  Pallas kernels: 122 us -> 124 us
    pallas_call x1, Pallas kernels: 119 us -> 121 us  [body(): pl.pallas_call(partial(kernel, (leaves, rows, cols, group, ns, kb, cb, ro...]
where the time goes in v6:
time: 126 us; the launch traced here: 125 us
  Pallas kernels  124 us (98%)
    pallas_call x1, Pallas kernels, body(): pl.pallas_call(partial(kernel, (leaves, rows, cols, group, ns, kb, cb, ro...  121 us
    pallas_call x1, Pallas kernels, body(): pl.pallas_call(hand_over, out_shape=tuple((jax.ShapeDtypeStruct(one.shape...  2.57 us

profile of v6, /device:TPU:231, one launch (start us, length us, event | category | flops | bytes accessed | tf_op | source)
XLA Modules:
  0.0 124.5 jit_solution(16037186431609991889)
XLA Ops:
  0.6 121.3 %shard_map.59 = (f32[2,256,256]{2,1,0:T(8,128)}, f32[2,512,256]{2,1,0:T(8,128)}) custom-call(f32[2,1024,512]{2,1,0:T(8,128)} %w_hbm.1, f32[2,512,256]{2,1,0:T(8,128)} %i_ref.1, f32[1024,256]{1,0:T(8,128)} %sig_hbm.1, s32[16,1024]{1,0:T(8,128)} %st_ref.1), custom_call_target="tpu_custom_call" | custom-call | tf_op jit(solution)/shard_map/pallas_call | solution.py:543
  122.0 2.6 %shard_map.60 = (f32[2,256,256]{2,1,0:T(8,128)}, f32[2,512,256]{2,1,0:T(8,128)}) custom-call(f32[2,256,256]{2,1,0:T(8,128)} %get-tuple-element.4.sp_in, f32[2,512,256]{2,1,0:T(8,128)} %get-tuple-element.5.sd_in), custom_call_target="tpu_custom_call" | custom-call | tf_op jit(solution)/shard_map/pallas_call | solution.py:586

commit v7 on v5

--- a/solution.py
+++ b/solution.py
@@ -433,6 +433,9 @@
     ig[c] = i_ref[...]
     product_partial(0)
     pick()
+    product_partial(1)
+    for h in range(group):
+        it[h] = i_ref[h].T
     pl.semaphore_wait(barrier, 2 + leaves + (z > 0).astype(jnp.int32) + (z < depth - 1).astype(jnp.int32)
         + 2 * corner.astype(jnp.int32))
     for one in exchange:
@@ -446,7 +449,6 @@
     rs_arrived(p0)
     product_done(0)
     ag_round1(f0)
-    product_partial(1)
     rs_round1(p1)
     for one in exchange:
         one.wait_recv()
@@ -469,8 +471,6 @@
     ag_round2(f1)
     z_relay(3, 2)
     ag_round2(q0)
-    for h in range(group):
-        it[h] = i_ref[h].T
     z_relay(3, 3)
     ag_arrived(f1)
     z_last(3)

time: 124 us -> 125 us (level); the launches traced: 122 us -> 125 us
  Pallas kernels: 122 us -> 124 us
    pallas_call x1, Pallas kernels: 119 us -> 122 us  [body(): pl.pallas_call(partial(kernel, (leaves, rows, cols, group, ns, kb, cb, ro...]
where the time goes in v7:
time: 125 us
  Pallas kernels  124 us (99%)
    pallas_call x1, Pallas kernels, body(): pl.pallas_call(partial(kernel, (leaves, rows, cols, group, ns, kb, cb, ro...  122 us
    pallas_call x1, Pallas kernels, body(): pl.pallas_call(hand_over, out_shape=tuple((jax.ShapeDtypeStruct(one.shape...  2.57 us

profile of v7, /device:TPU:231, one launch (start us, length us, event | category | flops | bytes accessed | tf_op | source)
XLA Modules:
  0.0 124.7 jit_solution(13823290731977312032)
XLA Ops:
  0.6 121.5 %shard_map.59 = (f32[2,256,256]{2,1,0:T(8,128)}, f32[2,512,256]{2,1,0:T(8,128)}) custom-call(f32[2,1024,512]{2,1,0:T(8,128)} %w_hbm.1, f32[2,512,256]{2,1,0:T(8,128)} %i_ref.1, f32[1024,256]{1,0:T(8,128)} %sig_hbm.1, s32[16,1024]{1,0:T(8,128)} %st_ref.1), custom_call_target="tpu_custom_call" | custom-call | tf_op jit(solution)/shard_map/pallas_call | solution.py:534
  122.2 2.6 %shard_map.60 = (f32[2,256,256]{2,1,0:T(8,128)}, f32[2,512,256]{2,1,0:T(8,128)}) custom-call(f32[2,256,256]{2,1,0:T(8,128)} %get-tuple-element.4.sp_in, f32[2,512,256]{2,1,0:T(8,128)} %get-tuple-element.5.sd_in), custom_call_target="tpu_custom_call" | custom-call | tf_op jit(solution)/shard_map/pallas_call | solution.py:577
